TPU v7x, 32 devices: a whole 2x2x4 slice. The times are simulated.
32 devices in a mesh: pair: 4 (over y, x), col: 8 (over z, core).
Axes of the slice: x: 2, y: 2, z: 4, core: 2. Of those that a mesh axis runs over, the one named last changes fastest.
Arguments:
- amplitudes: float32 [2048, 2048], P('pair', 'col'), may hold values from -6 to 6
- integrals: float32 [2048, 2048], P('pair', 'col'), may hold values from -0.25 to 0.25
- amp_tiles: int32 [4, 8, 4], P('pair', 'col'), may hold values from 0 to 7, as said below
- amp_count: int32 [4, 8], P('pair', 'col'), may hold values from 1 to 4, as said below
- int_mask: int32 [16, 16], P('pair', 'col'), may hold values 0 or 1
Outputs:
- ladder: float32 [2048, 2048], P('pair', 'col')
Inputs may be any that keep to these rules, and one draw needn't show every extreme that they name: `amp_tiles`: in each device's list the entries are distinct tile numbers of that device's block. `amp_count`: some device's count equals 4 in every draw.
All inputs are finite; a program needn't handle non-finite values. No bound on the sum of `int_mask` on one device may be relied on, other than what follows from the above.
Results may differ from a plain program's by a relative error of at most 0.00007.
Values sent between devices are 32-bit elements; how exact they have to be, the bound alone decides.
A program may use at most 128 MiB of HBM per device.

v0:
```python
import functools

import jax
import jax.numpy as jnp
from jax import lax
from jax.experimental import pallas as pl
from jax.experimental.pallas import tpu as pltpu
from jax.sharding import PartitionSpec as P

TILE = 128
CORES = 2
VMEM_BYTES = 60 << 20
MESH = pl.DeviceIdType.MESH
BF16 = jnp.bfloat16
F32 = jnp.float32


def split(value):
    high = value.astype(BF16)
    return high, (value - high.astype(F32)).astype(BF16)


def when(*conditions):
    together = conditions[0]
    for condition in conditions[1:]:
        together = jnp.logical_and(together, condition)
    return pl.when(together)


def kernel(
    n_pair, n_col, list_hbm, count_hbm, mask_hbm, amp_hbm, int_hbm, out_ref,
    list_ref, count_ref, mask_ref, place_ref, amp, part_high, part_low, packed, slots, ints, a_high, a_low, b_high, b_low,
    load_small, load_amp, load_int, load_place, amp_recv, amp_send, slot_recv, slot_send, int_recv, int_send,
):
    live = packed.shape[1]
    rows, depth = a_high.shape[1:]
    tile_cols = depth // TILE
    tiles = amp.shape[0]
    int_rows, int_cols = ints.shape[1:]
    half = int_rows // 2
    piece = TILE
    pieces = half // piece

    pair, col = lax.axis_index("pair"), lax.axis_index("col")
    line, line_at, core = n_col // CORES, col // CORES, col % CORES
    wide = n_pair // 2
    high_at, low_at = pair // wide, pair % wide

    sibling = {"col": line_at * CORES + 1 - core}
    above, below = {"col": col + CORES}, {"col": col - CORES}
    across = {"pair": (1 - high_at) * wide + low_at}
    right, left = {"pair": pair + 1}, {"pair": pair - 1}
    has_above, has_below = line_at < line - 1, line_at > 0
    has_right, has_left = low_at < wide - 1, low_at > 0

    int_loads = [
        pltpu.make_async_copy(
            int_hbm.at[pl.ds(at * piece, piece)],
            ints.at[pair, pl.ds(at * piece, piece)],
            load_int.at[at],
        )
        for at in range(2 * pieces)
    ]
    small_loads = [
        pltpu.make_async_copy(source, target, load_small.at[at])
        for at, (source, target) in enumerate(
            ((list_hbm, list_ref), (count_hbm, count_ref), (mask_hbm, mask_ref))
        )
    ]
    def tile_at(t):
        return pl.ds(t // tile_cols * TILE, TILE), pl.ds(t % tile_cols * TILE, TILE)

    amp_loads = [
        pltpu.make_async_copy(amp_hbm.at[tile_at(t)], amp.at[t], load_amp.at[t])
        for t in range(tiles)
    ]
    for load in small_loads:
        load.start()
    for load in amp_loads:
        load.start()
    for load in int_loads:
        load.start()

    barrier = pltpu.get_barrier_semaphore()
    partners = (
        (sibling, None), (across, None), (above, has_above), (below, has_below),
        (right, has_right), (left, has_left),
    )
    for partner, exists in partners:
        def greet(partner=partner):
            pl.semaphore_signal(barrier, inc=1, device_id=partner, device_id_type=MESH)
        if exists is None:
            greet()
        else:
            pl.when(exists)(greet)
    groups = [(0, 1), (1, live - 1)] if live > 1 else [(0, 1)]

    def amp_copy(source, slot, way, target):
        first, count = groups[slot]
        ref = packed.at[source, pl.ds(first, count)]
        return pltpu.make_async_remote_copy(
            src_ref=ref, dst_ref=ref,
            send_sem=amp_send.at[way, source, slot], recv_sem=amp_recv.at[source, slot],
            device_id=target, device_id_type=MESH,
        )

    def slot_copy(source, way, target):
        ref = slots.at[source]
        return pltpu.make_async_remote_copy(
            src_ref=ref, dst_ref=ref,
            send_sem=slot_send.at[way, source], recv_sem=slot_recv.at[source],
            device_id=target, device_id_type=MESH,
        )

    def int_copy(source, at, way, target, count=1):
        ref = ints.at[source, pl.ds(at * piece, count * piece)]
        return pltpu.make_async_remote_copy(
            src_ref=ref, dst_ref=ref,
            send_sem=int_send.at[way, source, at], recv_sem=int_recv.at[source, at],
            device_id=target, device_id_type=MESH,
        )

    def place_copy(source):
        return pltpu.make_async_copy(
            slots.at[source], place_ref.at[source], load_place.at[source]
        )

    out_ref[...] = jnp.zeros_like(out_ref)
    part_high[live] = jnp.zeros((TILE, TILE), BF16)
    part_low[live] = jnp.zeros((TILE, TILE), BF16)
    for load in small_loads:
        load.wait()
    numbers = [
        jnp.where(
            jnp.full((1, TILE), count_ref[0, 0], jnp.int32) > s,
            jnp.full((1, TILE), list_ref[0, 0, s], jnp.int32),
            -1,
        )
        for s in range(live)
    ]
    for t in range(tiles):
        place = jnp.full((1, TILE), live, jnp.int32)
        for s in range(live):
            place = jnp.where(numbers[s] == t, s, place)
        slots[col, pl.ds(t, 1), :] = place
    place_copy(col).start()
    for load in amp_loads:
        load.wait()
    for s in range(live):
        packed[col, s] = amp[list_ref[0, 0, s]]

    for at in range(2 * pieces):
        int_loads[at].wait()
        span = pl.ds(at * piece, piece)
        for c in range(int_cols // TILE):
            keep = mask_ref[c, at * piece // TILE].astype(F32)
            cols = pl.ds(c * TILE, TILE)
            ints[pair, span, cols] = ints[pair, span, cols] * keep

    peers = 2
    for _, exists in partners[2:]:
        peers += jnp.where(exists, 1, 0)
    pl.semaphore_wait(barrier, peers)

    def send_own_amp(copy):
        pl.when(has_above)(lambda: copy(0, above).start())
        pl.when(has_below)(lambda: copy(1, below).start())
        copy(2, sibling).start()

    def send_row(source, at, count=1):
        pl.when(has_right)(lambda: int_copy(source, at, 0, right, count).start())
        pl.when(has_left)(lambda: int_copy(source, at, 1, left, count).start())

    send_own_amp(lambda way, target: slot_copy(col, way, target))
    for s in range(max(len(groups), pieces)):
        if s < len(groups):
            send_own_amp(lambda way, target, s=s: amp_copy(col, s, way, target))
        if s < pieces:
            send_row(pair, s)
            int_copy(pair, pieces + s, 2, across).start()
    send_row(pair, pieces, pieces)
    int_copy(pair, 0, 2, across, pieces).start()

    def amp_slot(source):
        return jnp.abs(source // CORES - line_at)

    def int_slot(source, part):
        away = jnp.abs(source % wide - low_at)
        same = source // wide == high_at
        near = jnp.where(part == 0, away, jnp.where(away > 0, away + 1, 0))
        far = jnp.where(part == 0, away + 2, jnp.where(away > 0, away + 2, 1))
        return jnp.where(same, near, far)

    def step(now, _):
        def pass_amp(source, exists, way, target, more):
            @when(now >= 1, exists)
            def _():
                slot_copy(source, way, target).wait_recv()
                place_copy(source).start()
                pl.when(more)(lambda: slot_copy(source, way, target).start())
                slot_copy(source, 2, sibling).start()

        def pass_tile(source, s, exists, way, target, more):
            @when(now >= 1, exists)
            def _():
                amp_copy(source, s, way, target).wait_recv()
                pl.when(more)(lambda: amp_copy(source, s, way, target).start())
                amp_copy(source, s, 2, sibling).start()

        def pass_row(source, at, away, across_too, count=1):
            def one(side, exists, way, target, more):
                origin = source + side * away

                @when(away >= 1, exists)
                def _():
                    int_copy(origin, at, way, target, count).wait_recv()
                    pl.when(more)(lambda: int_copy(origin, at, way, target, count).start())
                    if across_too:
                        int_copy(origin, at, 2, across).start()

            one(-1, low_at - away >= 0, 0, right, has_right)
            one(1, low_at + away < wide, 1, left, has_left)

        lower, upper = col - CORES * now, col + CORES * now
        pass_amp(lower, line_at - now >= 0, 0, above, has_above)
        pass_amp(upper, line_at + now < line, 1, below, has_below)
        other = (1 - high_at) * wide + low_at
        for s in range(max(len(groups), pieces)):
            if s < len(groups):
                pass_tile(lower, s, line_at - now >= 0, 0, above, has_above)
                pass_tile(upper, s, line_at + now < line, 1, below, has_below)
            if s < pieces:
                pass_row(pair, s, now, True)

                @when(now == 1)
                def _(s=s):
                    int_copy(other, pieces + s, 2, across).wait_recv()
                    send_row(other, pieces + s)

        away = now - 2
        pass_row(pair, pieces, now - 1, False, pieces)
        pl.when(away == 0)(lambda: int_copy(other, 0, 2, across, pieces).wait_recv())
        for u in range(pieces):
            pass_row(other, pieces + u, away, False)
            for side, exists in ((-1, low_at - away >= 0), (1, low_at + away < wide)):
                @when(away >= 1, exists)
                def _(side=side, u=u):
                    int_copy(other + side * away, u, 2, across).wait_recv()

        def from_sibling(source):
            slot_copy(source, 2, sibling).wait_recv()
            place_copy(source).start()
            for s in range(len(groups)):
                amp_copy(source, s, 2, sibling).wait_recv()

        @pl.loop(0, n_pair * 2)
        def _(block):
            source, part = block // 2, block % 2

            @pl.when(int_slot(source, part) == now)
            def _():
                span = pl.ds(pl.multiple_of(part * half, half), half)
                value = ints[source, span]
                b_high[source, span], b_low[source, span] = split(value)

        mate = line_at * CORES + 1 - core

        @pl.loop(0, CORES)
        def _(turn):
            @pl.when(turn == 1)
            def _():
                pl.when(line_at - now >= 0)(lambda: from_sibling(mate - CORES * now))
                when(now >= 1, line_at + now < line)(lambda: from_sibling(mate + CORES * now))

            @pl.loop(0, line)
            def _(place_at):
                source = place_at * CORES + (core + turn) % CORES

                @pl.when(amp_slot(source) == now)
                def _():
                    for s in range(live):
                        part_high[s], part_low[s] = split(packed[source, s])
                    place_copy(source).wait()
                    for t in range(tiles):
                        place = place_ref[source, t, 0]
                        a_high[(source, *tile_at(t))] = part_high[place]
                        a_low[(source, *tile_at(t))] = part_low[place]

                start = source * depth
                origin, offset = start // int_rows, start % int_rows
                due = jnp.maximum(amp_slot(source), int_slot(origin, offset // half))

                @pl.when(due == now)
                def _():
                    span = pl.ds(pl.multiple_of(offset, depth), depth)
                    high, low = b_high[origin, span], b_low[origin, span]
                    first = a_high[source]
                    total = jnp.dot(first, high, preferred_element_type=F32)
                    total += jnp.dot(first, low, preferred_element_type=F32)
                    total += jnp.dot(a_low[source], high, preferred_element_type=F32)
                    out_ref[...] += total

        return 0

    steps = max(line - 1, wide + 1)
    lax.fori_loop(0, steps + 1, step, 0)

    @pl.loop(0, n_col)
    def _(source):
        mine = source % CORES == core
        at = source // CORES

        def drain(way, target):
            slot_copy(source, way, target).wait_send()
            for s in range(len(groups)):
                amp_copy(source, s, way, target).wait_send()

        when(mine, at <= line_at, has_above)(lambda: drain(0, above))
        when(mine, at >= line_at, has_below)(lambda: drain(1, below))
        pl.when(mine)(lambda: drain(2, sibling))

    @pl.loop(0, n_pair)
    def _(source):
        same = source // wide == high_at
        at = source % wide

        def drain(first, way, target, count=1):
            for u in range(0, pieces, count):
                int_copy(source, first + u, way, target, count).wait_send()

        to_right, to_left = (at <= low_at, has_right), (at >= low_at, has_left)
        when(same, *to_right)(lambda: drain(0, 0, right))
        when(same, *to_left)(lambda: drain(0, 1, left))
        when(same, at != low_at)(lambda: drain(0, 2, across))
        when(same, at == low_at)(lambda: drain(0, 2, across, pieces))
        when(same, *to_right)(lambda: drain(pieces, 0, right, pieces))
        when(same, *to_left)(lambda: drain(pieces, 1, left, pieces))
        when(~same, *to_right)(lambda: drain(pieces, 0, right))
        when(~same, *to_left)(lambda: drain(pieces, 1, left))
        pl.when(source == pair)(lambda: drain(pieces, 2, across))


def local(n_pair, n_col, amplitudes, integrals, amp_tiles, amp_count, int_mask):
    rows, depth = amplitudes.shape
    int_rows, int_cols = integrals.shape
    live = amp_tiles.shape[-1]
    tiles = (rows // TILE) * (depth // TILE)
    half = int_rows // 2
    assert n_pair % 2 == 0 and n_col % CORES == 0
    assert half % depth == 0 and half % TILE == 0
    pieces = int_rows // TILE
    scratch = [
        pltpu.SMEM(amp_tiles.shape, jnp.int32),
        pltpu.SMEM(amp_count.shape, jnp.int32),
        pltpu.SMEM(int_mask.shape[::-1], jnp.int32),
        pltpu.SMEM((n_col, tiles, TILE), jnp.int32),
        pltpu.VMEM((tiles, TILE, TILE), F32),
        pltpu.VMEM((live + 1, TILE, TILE), BF16),
        pltpu.VMEM((live + 1, TILE, TILE), BF16),
        pltpu.VMEM((n_col, live, TILE, TILE), F32),
        pltpu.VMEM((n_col, tiles, TILE), jnp.int32),
        pltpu.VMEM((n_pair, int_rows, int_cols), F32),
        pltpu.VMEM((n_col, rows, depth), BF16),
        pltpu.VMEM((n_col, rows, depth), BF16),
        pltpu.VMEM((n_pair, int_rows, int_cols), BF16),
        pltpu.VMEM((n_pair, int_rows, int_cols), BF16),
        pltpu.SemaphoreType.DMA((3,)),
        pltpu.SemaphoreType.DMA((tiles,)),
        pltpu.SemaphoreType.DMA((pieces,)),
        pltpu.SemaphoreType.DMA((n_col,)),
        pltpu.SemaphoreType.DMA((n_col, live)),
        pltpu.SemaphoreType.DMA((3, n_col, live)),
        pltpu.SemaphoreType.DMA((n_col,)),
        pltpu.SemaphoreType.DMA((3, n_col)),
        pltpu.SemaphoreType.DMA((n_pair, pieces)),
        pltpu.SemaphoreType.DMA((3, n_pair, pieces)),
    ]
    return pl.pallas_call(
        functools.partial(kernel, n_pair, n_col),
        out_shape=pltpu.VMEM((rows, int_cols), F32),
        in_specs=[pl.BlockSpec(memory_space=pltpu.HBM)] * 5,
        out_specs=pl.BlockSpec(memory_space=pltpu.VMEM),
        scratch_shapes=scratch,
        compiler_params=pltpu.CompilerParams(
            collective_id=0, has_side_effects=True, vmem_limit_bytes=VMEM_BYTES
        ),
        cost_estimate=pl.CostEstimate(
            flops=6 * rows * depth * n_col * int_cols,
            bytes_accessed=4 * rows * (2 * depth + int_cols),
            transcendentals=0,
        ),
        name="ladder",
    )(amp_tiles, amp_count, int_mask.T, amplitudes, integrals)


def solution(mesh):
    return jax.shard_map(
        functools.partial(local, mesh.shape["pair"], mesh.shape["col"]),
        mesh=mesh,
        in_specs=(
            P("pair", "col"),
            P("pair", "col"),
            P("pair", "col", None),
            P("pair", "col"),
            P("pair", "col"),
        ),
        out_specs=P("pair", "col"),
        check_vma=False,
    )
```

profile of v0, /device:TPU:0, one launch (start us, length us, event | category | flops | bytes accessed | tf_op | source)
XLA Modules:
  0.0 28.5 jit_solution(6995307163329962442)
XLA Ops:
  0.7 27.0 %ladder.1 = f32[512,256]{1,0:T(8,128)S(1)} custom-call(s32[1,1,4]{2,1,0:T(1,128)} %list_hbm.1, s32[1,1]{1,0:T(1,128)S(6)} %copy.8.count_hbm, s32[2,4]{1,0:T(2,128)} %bitcast.1, f32[512,256]{1,0:T(8,128)} %amp_hbm.1, f32[512,256]{1,0:T(8,128)} %int_hbm.1), custom_call_target="tpu_custom_call" | custom-call | flops 1610612736 | bytes 1572864 | tf_op jit(solution)/shard_map/ladder/pallas_call | solution.py:378
  27.7 0.8 %copy.7 = f32[512,256]{1,0:T(8,128)} copy(f32[512,256]{1,0:T(8,128)S(1)} %ladder.1) | data formatting | bytes 1048576
where the time goes:
time: 28.6 us; the launch traced here: 28.5 us
  Pallas kernels  27 us (94%)
  local copies, waits for them, and re-layouts  0.8 us (3%)
  between operations  0.66 us (2%)
    pallas_call x1, Pallas kernels, local(): pl.pallas_call(functools.partial(kernel, n_pair, n_col), out_shape=pltpu....  27 us
    unnamed x1, local copies, waits for them, and re-layouts  0.8 us

commit v1 on v0

--- a/solution.py
+++ b/solution.py
@@ -18,6 +18,14 @@
 def split(value):
     high = value.astype(BF16)
     return high, (value - high.astype(F32)).astype(BF16)
+
+
+def div(value, by):
+    return lax.div(value, jnp.int32(by))
+
+
+def rem(value, by):
+    return lax.rem(value, jnp.int32(by))
 
 
 def when(*conditions):
@@ -125,7 +133,6 @@
             slots.at[source], place_ref.at[source], load_place.at[source]
         )
 
-    out_ref[...] = jnp.zeros_like(out_ref)
     part_high[live] = jnp.zeros((TILE, TILE), BF16)
     part_low[live] = jnp.zeros((TILE, TILE), BF16)
     for load in small_loads:
@@ -181,17 +188,58 @@
     send_row(pair, pieces, pieces)
     int_copy(pair, 0, 2, across, pieces).start()
 
+    out_ref[...] = jnp.zeros_like(out_ref)
+
     def amp_slot(source):
-        return jnp.abs(source // CORES - line_at)
+        return jnp.abs(div(source, CORES) - line_at)
 
     def int_slot(source, part):
-        away = jnp.abs(source % wide - low_at)
-        same = source // wide == high_at
+        away = jnp.abs(rem(source, wide) - low_at)
+        same = div(source, wide) == high_at
         near = jnp.where(part == 0, away, jnp.where(away > 0, away + 1, 0))
         far = jnp.where(part == 0, away + 2, jnp.where(away > 0, away + 2, 1))
         return jnp.where(same, near, far)
 
+    steps = max(line - 1, wide + 1)
+
+    def drain_amp(source, way, target):
+        slot_copy(source, way, target).wait_send()
+        for s in range(len(groups)):
+            amp_copy(source, s, way, target).wait_send()
+
+    def drain_early():
+        @pl.loop(0, n_col)
+        def _(source):
+            mine = rem(source, CORES) == core
+            at = div(source, CORES)
+
+            when(mine, at <= line_at, has_above)(lambda: drain_amp(source, 0, above))
+            when(mine, at >= line_at, has_below)(lambda: drain_amp(source, 1, below))
+            when(mine, jnp.abs(at - line_at) < steps)(lambda: drain_amp(source, 2, sibling))
+
+        @pl.loop(0, n_pair)
+        def _(source):
+            same = div(source, wide) == high_at
+            at = rem(source, wide)
+
+            def drain(first, way, target, count=1):
+                for u in range(0, pieces, count):
+                    int_copy(source, first + u, way, target, count).wait_send()
+
+            to_right, to_left = (at <= low_at, has_right), (at >= low_at, has_left)
+            when(same, *to_right)(lambda: drain(0, 0, right))
+            when(same, *to_left)(lambda: drain(0, 1, left))
+            when(same, at != low_at)(lambda: drain(0, 2, across))
+            when(same, at == low_at)(lambda: drain(0, 2, across, pieces))
+            when(same, *to_right)(lambda: drain(pieces, 0, right, pieces))
+            when(same, *to_left)(lambda: drain(pieces, 1, left, pieces))
+            when(~same, *to_right)(lambda: drain(pieces, 0, right))
+            when(~same, *to_left)(lambda: drain(pieces, 1, left))
+            pl.when(source == pair)(lambda: drain(pieces, 2, across))
+
     def step(now, _):
+        pl.when(now == steps)(drain_early)
+
         def pass_amp(source, exists, way, target, more):
             @when(now >= 1, exists)
             def _():
@@ -255,7 +303,7 @@
 
         @pl.loop(0, n_pair * 2)
         def _(block):
-            source, part = block // 2, block % 2
+            source, part = div(block, 2), rem(block, 2)
 
             @pl.when(int_slot(source, part) == now)
             def _():
@@ -272,11 +320,14 @@
                 pl.when(line_at - now >= 0)(lambda: from_sibling(mate - CORES * now))
                 when(now >= 1, line_at + now < line)(lambda: from_sibling(mate + CORES * now))
 
-            @pl.loop(0, line)
-            def _(place_at):
-                source = place_at * CORES + (core + turn) % CORES
-
-                @pl.when(amp_slot(source) == now)
+            other_core = rem(core + turn, CORES)
+
+            @pl.loop(0, 2)
+            def _(side):
+                place_at = line_at + (2 * side - 1) * now
+                source = place_at * CORES + other_core
+
+                @when(place_at >= 0, place_at < line, (side == 0) | (now > 0))
                 def _():
                     for s in range(live):
                         part_high[s], part_low[s] = split(packed[source, s])
@@ -286,9 +337,12 @@
                         a_high[(source, *tile_at(t))] = part_high[place]
                         a_low[(source, *tile_at(t))] = part_low[place]
 
+            @pl.loop(0, line)
+            def _(place_at):
+                source = place_at * CORES + other_core
                 start = source * depth
-                origin, offset = start // int_rows, start % int_rows
-                due = jnp.maximum(amp_slot(source), int_slot(origin, offset // half))
+                origin, offset = div(start, int_rows), rem(start, int_rows)
+                due = jnp.maximum(amp_slot(source), int_slot(origin, div(offset, half)))
 
                 @pl.when(due == now)
                 def _():
@@ -302,42 +356,14 @@
 
         return 0
 
-    steps = max(line - 1, wide + 1)
     lax.fori_loop(0, steps + 1, step, 0)
 
-    @pl.loop(0, n_col)
-    def _(source):
-        mine = source % CORES == core
-        at = source // CORES
-
-        def drain(way, target):
-            slot_copy(source, way, target).wait_send()
-            for s in range(len(groups)):
-                amp_copy(source, s, way, target).wait_send()
-
-        when(mine, at <= line_at, has_above)(lambda: drain(0, above))
-        when(mine, at >= line_at, has_below)(lambda: drain(1, below))
-        pl.when(mine)(lambda: drain(2, sibling))
-
-    @pl.loop(0, n_pair)
-    def _(source):
-        same = source // wide == high_at
-        at = source % wide
-
-        def drain(first, way, target, count=1):
-            for u in range(0, pieces, count):
-                int_copy(source, first + u, way, target, count).wait_send()
-
-        to_right, to_left = (at <= low_at, has_right), (at >= low_at, has_left)
-        when(same, *to_right)(lambda: drain(0, 0, right))
-        when(same, *to_left)(lambda: drain(0, 1, left))
-        when(same, at != low_at)(lambda: drain(0, 2, across))
-        when(same, at == low_at)(lambda: drain(0, 2, across, pieces))
-        when(same, *to_right)(lambda: drain(pieces, 0, right, pieces))
-        when(same, *to_left)(lambda: drain(pieces, 1, left, pieces))
-        when(~same, *to_right)(lambda: drain(pieces, 0, right))
-        when(~same, *to_left)(lambda: drain(pieces, 1, left))
-        pl.when(source == pair)(lambda: drain(pieces, 2, across))
+    for side in (-1, 1):
+        ending = line_at + side * steps
+
+        @when(ending >= 0, ending < line)
+        def _(ending=ending):
+            drain_amp(ending * CORES + core, 2, sibling)
 
 
 def local(n_pair, n_col, amplitudes, integrals, amp_tiles, amp_count, int_mask):

time: 28.6 us -> 28.3 us (0.990)
  Pallas kernels: 27 us -> 26.7 us
    pallas_call x1, Pallas kernels: 27 us -> 26.7 us  [local(): pl.pallas_call(functools.partial(kernel, n_pair, n_col), out_shape=pltpu....]
where the time goes in v1:
time: 28.3 us; the launch traced here: 28.1 us
  Pallas kernels  26.7 us (94%)
  local copies, waits for them, and re-layouts  0.8 us (3%)
  between operations  0.66 us (2%)
    pallas_call x1, Pallas kernels, local(): pl.pallas_call(functools.partial(kernel, n_pair, n_col), out_shape=pltpu....  26.7 us
    unnamed x1, local copies, waits for them, and re-layouts  0.8 us

profile of v1, /device:TPU:0, one launch (start us, length us, event | category | flops | bytes accessed | tf_op | source)
XLA Modules:
  0.0 28.1 jit_solution(11593274292673529650)
XLA Ops:
  0.7 26.7 %ladder.1 = f32[512,256]{1,0:T(8,128)S(1)} custom-call(s32[1,1,4]{2,1,0:T(1,128)} %list_hbm.1, s32[1,1]{1,0:T(1,128)S(6)} %copy.8.count_hbm, s32[2,4]{1,0:T(2,128)} %bitcast.1, f32[512,256]{1,0:T(8,128)} %amp_hbm.1, f32[512,256]{1,0:T(8,128)} %int_hbm.1), custom_call_target="tpu_custom_call" | custom-call | flops 1610612736 | bytes 1572864 | tf_op jit(solution)/shard_map/ladder/pallas_call | solution.py:404
  27.3 0.8 %copy.7 = f32[512,256]{1,0:T(8,128)} copy(f32[512,256]{1,0:T(8,128)S(1)} %ladder.1) | data formatting | bytes 1048576

commit v2 on v1

--- a/solution.py
+++ b/solution.py
@@ -349,10 +349,11 @@
                     span = pl.ds(pl.multiple_of(offset, depth), depth)
                     high, low = b_high[origin, span], b_low[origin, span]
                     first = a_high[source]
-                    total = jnp.dot(first, high, preferred_element_type=F32)
-                    total += jnp.dot(first, low, preferred_element_type=F32)
-                    total += jnp.dot(a_low[source], high, preferred_element_type=F32)
-                    out_ref[...] += total
+                    out_ref[...] += jnp.dot(
+                        jnp.concatenate([first, a_low[source], first], axis=1),
+                        jnp.concatenate([high, high, low], axis=0),
+                        preferred_element_type=F32,
+                    )
 
         return 0
 

time: 28.3 us -> 28.3 us (level)
  no operation moved by 1% of the time
where the time goes in v2:
time: 28.3 us; the launch traced here: 28.1 us
  Pallas kernels  26.7 us (94%)
  local copies, waits for them, and re-layouts  0.8 us (3%)
  between operations  0.66 us (2%)
    pallas_call x1, Pallas kernels, local(): pl.pallas_call(functools.partial(kernel, n_pair, n_col), out_shape=pltpu....  26.7 us
    unnamed x1, local copies, waits for them, and re-layouts  0.8 us

profile of v2, /device:TPU:0, one launch (start us, length us, event | category | flops | bytes accessed | tf_op | source)
XLA Modules:
  0.0 28.1 jit_solution(15393054413085306219)
XLA Ops:
  0.7 26.7 %ladder.1 = f32[512,256]{1,0:T(8,128)S(1)} custom-call(s32[1,1,4]{2,1,0:T(1,128)} %list_hbm.1, s32[1,1]{1,0:T(1,128)S(6)} %copy.8.count_hbm, s32[2,4]{1,0:T(2,128)} %bitcast.1, f32[512,256]{1,0:T(8,128)} %amp_hbm.1, f32[512,256]{1,0:T(8,128)} %int_hbm.1), custom_call_target="tpu_custom_call" | custom-call | flops 1610612736 | bytes 1572864 | tf_op jit(solution)/shard_map/ladder/pallas_call | solution.py:405
  27.3 0.8 %copy.7 = f32[512,256]{1,0:T(8,128)} copy(f32[512,256]{1,0:T(8,128)S(1)} %ladder.1) | data formatting | bytes 1048576

commit v3 on v1

--- a/solution.py
+++ b/solution.py
@@ -156,6 +156,24 @@
     for s in range(live):
         packed[col, s] = amp[list_ref[0, 0, s]]
 
+    peers = 2
+    for _, exists in partners[2:]:
+        peers += jnp.where(exists, 1, 0)
+    pl.semaphore_wait(barrier, peers)
+
+    def send_own_amp(copy):
+        pl.when(has_above)(lambda: copy(0, above).start())
+        pl.when(has_below)(lambda: copy(1, below).start())
+        copy(2, sibling).start()
+
+    def send_row(source, at, count=1):
+        pl.when(has_right)(lambda: int_copy(source, at, 0, right, count).start())
+        pl.when(has_left)(lambda: int_copy(source, at, 1, left, count).start())
+
+    send_own_amp(lambda way, target: slot_copy(col, way, target))
+    for s in range(len(groups)):
+        send_own_amp(lambda way, target, s=s: amp_copy(col, s, way, target))
+
     for at in range(2 * pieces):
         int_loads[at].wait()
         span = pl.ds(at * piece, piece)
@@ -164,27 +182,9 @@
             cols = pl.ds(c * TILE, TILE)
             ints[pair, span, cols] = ints[pair, span, cols] * keep
 
-    peers = 2
-    for _, exists in partners[2:]:
-        peers += jnp.where(exists, 1, 0)
-    pl.semaphore_wait(barrier, peers)
-
-    def send_own_amp(copy):
-        pl.when(has_above)(lambda: copy(0, above).start())
-        pl.when(has_below)(lambda: copy(1, below).start())
-        copy(2, sibling).start()
-
-    def send_row(source, at, count=1):
-        pl.when(has_right)(lambda: int_copy(source, at, 0, right, count).start())
-        pl.when(has_left)(lambda: int_copy(source, at, 1, left, count).start())
-
-    send_own_amp(lambda way, target: slot_copy(col, way, target))
-    for s in range(max(len(groups), pieces)):
-        if s < len(groups):
-            send_own_amp(lambda way, target, s=s: amp_copy(col, s, way, target))
-        if s < pieces:
-            send_row(pair, s)
-            int_copy(pair, pieces + s, 2, across).start()
+    for u in range(pieces):
+        send_row(pair, u)
+        int_copy(pair, pieces + u, 2, across).start()
     send_row(pair, pieces, pieces)
     int_copy(pair, 0, 2, across, pieces).start()
 

time: 28.3 us -> 28.3 us (level)
  no operation moved by 1% of the time
where the time goes in v3:
time: 28.3 us; the launch traced here: 28.1 us
  Pallas kernels  26.7 us (94%)
  local copies, waits for them, and re-layouts  0.8 us (3%)
  between operations  0.66 us (2%)
    pallas_call x1, Pallas kernels, local(): pl.pallas_call(functools.partial(kernel, n_pair, n_col), out_shape=pltpu....  26.7 us
    unnamed x1, local copies, waits for them, and re-layouts  0.8 us

profile of v3, /device:TPU:0, one launch (start us, length us, event | category | flops | bytes accessed | tf_op | source)
XLA Modules:
  0.0 28.1 jit_solution(17209252806886767872)
XLA Ops:
  0.7 26.7 %ladder.1 = f32[512,256]{1,0:T(8,128)S(1)} custom-call(s32[1,1,4]{2,1,0:T(1,128)} %list_hbm.1, s32[1,1]{1,0:T(1,128)S(6)} %copy.8.count_hbm, s32[2,4]{1,0:T(2,128)} %bitcast.1, f32[512,256]{1,0:T(8,128)} %amp_hbm.1, f32[512,256]{1,0:T(8,128)} %int_hbm.1), custom_call_target="tpu_custom_call" | custom-call | flops 1610612736 | bytes 1572864 | tf_op jit(solution)/shard_map/ladder/pallas_call | solution.py:404
  27.3 0.8 %copy.7 = f32[512,256]{1,0:T(8,128)} copy(f32[512,256]{1,0:T(8,128)S(1)} %ladder.1) | data formatting | bytes 1048576
